TPU v7x, 512 devices: a whole 4x8x8 slice. The times are simulated.
512 devices in a mesh: expert: 128 (over y, z, x_hi), hidden: 4 (over x_lo, core).
Axes of the slice: x: 4 (x_hi: 2, x_lo: 2; x = x_hi * 2 + x_lo), y: 8, z: 8, core: 2. Of those that a mesh axis runs over, the one named last changes fastest.
Arguments:
- tokens: bfloat16 [256, 256, 1280], P('expert', 'hidden'), may hold values from -400 to 400
- slot_embed: bfloat16 [128, 1280], replicated, may hold values from -1 to 1
- w_in: bfloat16 [128, 1280, 2560], P('expert', None, 'hidden'), may hold values from -0.15625 to 0.15625
- w_out: bfloat16 [128, 2560, 1280], P('expert', 'hidden'), may hold values from -0.125 to 0.125
- grad_out: bfloat16 [256, 256, 1280], P('expert', 'hidden'), may hold values from -96 to 96
Outputs:
- grad_tokens: bfloat16 [256, 256, 1280], P('expert', 'hidden')
- grad_embed: float32 [128, 1280], P('expert', 'hidden')
All inputs are finite; a program needn't handle non-finite values.
Results may differ from a plain program's by a relative error of at most 0.034.
Values may be sent and summed in bfloat16 or wider, within the bound.
A program may use at most 64 MiB of HBM per device.

v0:
```python
import jax
import jax.numpy as jnp
from jax import lax
from jax.sharding import PartitionSpec as P

half_root = 0.7071067811865476
density_scale = 0.3989422804014327


def gelu_slope(pre):
    return 0.5 * (1.0 + lax.erf(pre * half_root)) + pre * jnp.exp(-0.5 * pre * pre) * density_scale


def to_experts(parts):
    summed = lax.psum(parts.astype(jnp.bfloat16), "hidden")
    joined = lax.all_to_all(summed, "expert", split_axis=1, concat_axis=2, tiled=True)
    return joined.reshape(joined.shape[0], joined.shape[2], joined.shape[3])


def from_experts(parts):
    stacked = parts.reshape(parts.shape[0], lax.axis_size("expert"), -1, parts.shape[2])
    summed = lax.psum(stacked.astype(jnp.bfloat16), "hidden")
    return lax.all_to_all(summed, "expert", split_axis=1, concat_axis=1, tiled=True)


def expert_forward(rows, w_in, w_out):
    pre = jnp.dot(rows, w_in[0], preferred_element_type=jnp.float32)
    act = jax.nn.gelu(pre, approximate=False).astype(jnp.bfloat16)
    return (pre, jnp.dot(act, w_out[0], preferred_element_type=jnp.float32))


def expert_backward(pre, grads, w_in, w_out):
    contract = (((1,), (1,)), ((), ()))
    grad_act = lax.dot_general(grads, w_out[0], contract, preferred_element_type=jnp.float32)
    grad_pre = (grad_act * gelu_slope(pre)).astype(jnp.bfloat16)
    return lax.dot_general(grad_pre, w_in[0], contract, preferred_element_type=jnp.float32)


def shards(tokens, slot_embed, w_in, w_out, grad_out):
    logits = jnp.einsum("bmd,sd->bms", tokens, slot_embed, preferred_element_type=jnp.float32)
    column_top = lax.pmax(jnp.max(logits, axis=1), "hidden")
    column_exp = jnp.exp(logits - column_top[:, None, :])
    column_total = lax.psum(jnp.sum(column_exp, axis=1), "hidden")
    dispatch = column_exp / column_total[:, None, :]
    row_exp = jnp.exp(logits - jnp.max(logits, axis=2, keepdims=True))
    combine = row_exp / jnp.sum(row_exp, axis=2, keepdims=True)
    dispatch_low = dispatch.astype(jnp.bfloat16)
    combine_low = combine.astype(jnp.bfloat16)
    slot_part = jnp.einsum("bms,bmd->sbd", dispatch_low, tokens, preferred_element_type=jnp.float32)
    grad_part = jnp.einsum(
        "bms,bmd->sbd", combine_low, grad_out, preferred_element_type=jnp.float32
    )
    pre, out_part = expert_forward(to_experts(slot_part[None])[0], w_in, w_out)
    slot_out = from_experts(out_part[None])[0]
    grad_rows = to_experts(grad_part[None])[0]
    slot_grad = from_experts(expert_backward(pre, grad_rows, w_in, w_out)[None])[0]
    grad_comb = jnp.einsum("bmd,sbd->bms", grad_out, slot_out, preferred_element_type=jnp.float32)
    grad_disp = jnp.einsum("bmd,sbd->bms", tokens, slot_grad, preferred_element_type=jnp.float32)
    comb_inner = jnp.sum(combine * grad_comb, axis=2, keepdims=True)
    disp_inner = lax.psum(jnp.sum(dispatch * grad_disp, axis=1), "hidden")
    grad_logit = (
        combine * (grad_comb - comb_inner) + dispatch * (grad_disp - disp_inner[:, None, :])
    ).astype(jnp.bfloat16)
    grad_tokens = jnp.einsum(
        "bms,sbd->bmd", dispatch_low, slot_grad, preferred_element_type=jnp.float32
    ) + jnp.einsum("bms,sd->bmd", grad_logit, slot_embed, preferred_element_type=jnp.float32)
    embed_part = jnp.einsum("bms,bmd->sd", grad_logit, tokens, preferred_element_type=jnp.float32)
    embed_share = lax.psum_scatter(
        embed_part.reshape(-1), ("expert", "hidden"), scatter_dimension=0, tiled=True
    )
    return (grad_tokens.astype(jnp.bfloat16), embed_share.reshape(1, -1))


def solution(mesh):
    return jax.shard_map(
        shards,
        mesh=mesh,
        in_specs=(
            P("expert", "hidden", None),
            P(),
            P("expert", None, "hidden"),
            P("expert", "hidden", None),
            P("expert", "hidden", None),
        ),
        out_specs=(P("expert", "hidden", None), P("expert", "hidden")),
        check_vma=False,
    )
```

profile of v0, /device:TPU:1, one launch (start us, length us, event | category | flops | bytes accessed | tf_op | source)
XLA Modules:
  0.0 563.8 jit_solution(5319064201940134771)
XLA Ops:
  7.2 0.0 copy-start
  7.2 0.0 copy-start.6
  7.2 0.0 all-reduce.11.cloned.1.call-start
  7.2 1.5 fusion.67
  8.7 11.9 %pmax.7 = f32[2,128]{1,0:T(2,128)S(1)} all-reduce(f32[2,128]{1,0:T(2,128)S(1)} %get-tuple-element.8), channel_id=1, replica_groups=mesh['expert'=128,'hidden'=4] {'hidden'}, use_global_device_ids=true, to_apply=%region_1.0 | all-reduce | flops 256 | bytes 2048 | tf_op jit(solution)/shard_map/pmax | solution.py:41
  20.6 0.3 fusion.66
  21.0 5.8 %psum.42 = f32[2,128]{1,0:T(2,128)S(1)} all-reduce(f32[2,128]{1,0:T(2,128)S(1)} %fusion.56), channel_id=1, replica_groups=mesh['expert'=128,'hidden'=4] {'hidden'}, use_global_device_ids=true, to_apply=%region_3.0 | all-reduce | flops 256 | bytes 2048 | tf_op jit(solution)/shard_map/psum | solution.py:43
  26.8 2.2 fusion.3
  29.0 0.0 copy-done.6
  29.0 1.4 fusion.2
  30.4 0.0 all-reduce.11.cloned.1.call-update
  30.4 56.2 %all-reduce.11.cloned.1.call-done = (bf16[1,128,2,1280]{3,1,2,0:T(8,128)(2,1)}, bf16[1,128,2,1280]{3,1,2,0:T(8,128)(2,1)}) async-done(((bf16[1,128,2,1280]{3,1,2,0:T(8,128)(2,1)}, bf16[1,128,2,1280]{3,1,2,0:T(8,128)(2,1)}), (bf16[1,128,2,1280]{3,1,2,0:T(8,128)(2,1)}, bf16[1,128,2,1280]{3,1,2,0:T(8,128)(2,1)})) %all-reduce.11.cloned.1.call-update) | async-done | bytes 1310736 | tf_op jit(solution)/shard_map/psum | solution.py:15
  86.6 0.0 copy-start.4
  86.6 2.7 copy.14
  89.3 16.3 %all-to-all-start.1 = ((bf16[1,128,2,1280]{3,2,0,1:T(2,128)(2,1)}), bf16[1,128,2,1280]{3,2,0,1:T(2,128)(2,1)S(1)}, u32[]{:S(2)}, u32[]{:S(2)}) async-start(bf16[1,128,2,1280]{3,2,0,1:T(2,128)(2,1)} %copy.14), calls=%async_computation.1 | async-start | bytes 1310720 | tf_op jit(solution)/shard_map/all_to_all | solution.py:16
  105.6 0.0 copy-done.4
  105.6 1.5 copy.13
  107.1 20.3 %all-to-all-done.1 = bf16[1,128,2,1280]{3,2,0,1:T(2,128)(2,1)S(1)} async-done(((bf16[1,128,2,1280]{3,2,0,1:T(2,128)(2,1)}), bf16[1,128,2,1280]{3,2,0,1:T(2,128)(2,1)S(1)}, u32[]{:S(2)}, u32[]{:S(2)}) %all-to-all-start.1) | async-done | bytes 655392 | tf_op jit(solution)/shard_map/all_to_all | solution.py:16
  127.4 8.3 %all-to-all-start = ((bf16[1,128,2,1280]{3,2,0,1:T(2,128)(2,1)}), bf16[1,128,2,1280]{3,2,0,1:T(2,128)(2,1)S(1)}, u32[]{:S(2)}, u32[]{:S(2)}) async-start(bf16[1,128,2,1280]{3,2,0,1:T(2,128)(2,1)} %copy.13), calls=%async_computation | async-start | bytes 1310720 | tf_op jit(solution)/shard_map/all_to_all | solution.py:16
  135.7 0.0 all-reduce.9.cloned.1.call-start
  135.7 1.1 squeeze_reshape.7
  136.8 0.0 copy-done
  136.8 3.9 fusion.31
  140.7 15.8 %all-to-all-done = bf16[1,128,2,1280]{3,2,0,1:T(2,128)(2,1)S(1)} async-done(((bf16[1,128,2,1280]{3,2,0,1:T(2,128)(2,1)}), bf16[1,128,2,1280]{3,2,0,1:T(2,128)(2,1)S(1)}, u32[]{:S(2)}, u32[]{:S(2)}) %all-to-all-start) | async-done | bytes 655392 | tf_op jit(solution)/shard_map/all_to_all | solution.py:16
  156.5 0.2 squeeze_reshape.6
  156.8 2.3 fusion.16
  159.1 0.9 dot_general.49
  160.0 0.0 copy-start.2
  160.0 2.6 fusion.4
  162.6 1.8 dot_general.52
  164.4 0.0 copy-done.2
  164.4 2.5 fusion.5
  166.9 0.0 all-reduce.9.cloned.1.call-update
  166.9 50.4 %all-reduce.9.cloned.1.call-done = (bf16[1,128,2,1280]{3,1,2,0:T(8,128)(2,1)}, bf16[1,128,2,1280]{3,1,2,0:T(8,128)(2,1)}) async-done(((bf16[1,128,2,1280]{3,1,2,0:T(8,128)(2,1)}, bf16[1,128,2,1280]{3,1,2,0:T(8,128)(2,1)}), (bf16[1,128,2,1280]{3,1,2,0:T(8,128)(2,1)}, bf16[1,128,2,1280]{3,1,2,0:T(8,128)(2,1)})) %all-reduce.9.cloned.1.call-update) | async-done | bytes 1310736 | tf_op jit(solution)/shard_map/psum | solution.py:22
  217.3 0.0 copy-start.5
  217.3 2.7 copy.16
  220.0 16.5 %all-to-all-start.2 = ((bf16[1,128,2,1280]{3,2,0,1:T(2,128)(2,1)}), bf16[1,128,2,1280]{3,2,0,1:T(2,128)(2,1)S(1)}, u32[]{:S(2)}, u32[]{:S(2)}) async-start(bf16[1,128,2,1280]{3,2,0,1:T(2,128)(2,1)} %copy.16), calls=%async_computation.2 | async-start | bytes 1310720 | tf_op jit(solution)/shard_map/all_to_all | solution.py:23
  236.5 0.0 copy-start.1
  236.5 0.0 copy-done.5
  236.5 1.5 copy.19
  238.1 20.2 %all-to-all-done.2 = bf16[1,128,2,1280]{3,2,0,1:T(2,128)(2,1)S(1)} async-done(((bf16[1,128,2,1280]{3,2,0,1:T(2,128)(2,1)}), bf16[1,128,2,1280]{3,2,0,1:T(2,128)(2,1)S(1)}, u32[]{:S(2)}, u32[]{:S(2)}) %all-to-all-start.2) | async-done | bytes 655392 | tf_op jit(solution)/shard_map/all_to_all | solution.py:23
  258.3 8.3 %all-to-all-start.3 = ((bf16[1,128,2,1280]{3,2,0,1:T(2,128)(2,1)}), bf16[1,128,2,1280]{3,2,0,1:T(2,128)(2,1)S(1)}, u32[]{:S(2)}, u32[]{:S(2)}) async-start(bf16[1,128,2,1280]{3,2,0,1:T(2,128)(2,1)} %copy.19), calls=%async_computation.3 | async-start | bytes 1310720 | tf_op jit(solution)/shard_map/all_to_all | solution.py:23
  266.6 0.0 all-reduce.7.cloned.1.call-start
  266.6 0.0 copy-done.1
  266.6 0.4 multiply_reduce_fusion.1
  267.0 6.5 %psum.47 = f32[2,128]{1,0:T(2,128)S(1)} all-reduce(f32[2,128]{1,0:T(2,128)S(1)} %get-tuple-element.12), channel_id=1, replica_groups=mesh['expert'=128,'hidden'=4] {'hidden'}, use_global_device_ids=true, to_apply=%region_12.0 | all-reduce | flops 256 | bytes 2048 | tf_op jit(solution)/shard_map/psum | solution.py:60
  273.5 13.9 %all-to-all-done.3 = bf16[1,128,2,1280]{3,2,0,1:T(2,128)(2,1)S(1)} async-done(((bf16[1,128,2,1280]{3,2,0,1:T(2,128)(2,1)}), bf16[1,128,2,1280]{3,2,0,1:T(2,128)(2,1)S(1)}, u32[]{:S(2)}, u32[]{:S(2)}) %all-to-all-start.3) | async-done | bytes 655392 | tf_op jit(solution)/shard_map/all_to_all | solution.py:23
  287.4 1.3 convolution_bitcast_fusion.2
  288.7 0.6 convolution_bitcast_fusion
  289.3 0.9 reshape.32
  290.2 0.0 copy-start.3
  290.2 0.0 all-reduce.7.cloned.1.call-update
  290.2 0.2 fusion.34
  290.5 0.7 copy-done.3
  291.2 1.2 fusion.6
  292.3 263.6 %all-reduce.7.cloned.1.call-done = f32[163840]{0:T(1024)} async-done(((f32[163840]{0:T(1024)}), f32[163840]{0:T(1024)}) %all-reduce.7.cloned.1.call-update) | async-done | bytes 655376
  555.9 0.8 dynamic-slice
  556.7 0.6 reshape.33
  (1 shorter events, 0.0 us)
Async XLA Ops:
  7.2 129.7 %copy-start = (bf16[1,1280,640]{2,1,0:T(8,128)(2,1)S(1)}, bf16[1,1280,640]{2,1,0:T(8,128)(2,1)}, u32[]{:S(2)}) copy-start(bf16[1,1280,640]{2,1,0:T(8,128)(2,1)} %param.7) | copy-start | bytes 4915204
  7.2 21.8 %copy-start.6 = (bf16[2,64,1280]{2,1,0:T(8,128)(2,1)S(1)}, bf16[2,64,1280]{2,1,0:T(8,128)(2,1)}, u32[]{:S(2)}) copy-start(bf16[2,64,1280]{2,1,0:T(8,128)(2,1)} %param.9) | copy-start | bytes 983044
  7.2 79.4 %all-reduce.11.cloned.1.call-start = ((), (), s32[]{:S(2)}) async-start(), calls=%async_computation.6 | async-start | bytes 2621440 | tf_op jit(solution)/shard_map/psum | solution.py:15
  86.6 19.0 %copy-start.4 = (bf16[1,128,2,1280]{3,1,2,0:T(8,128)(2,1)S(1)}, bf16[1,128,2,1280]{3,1,2,0:T(8,128)(2,1)}, u32[]{:S(2)}) copy-start(bf16[1,128,2,1280]{3,1,2,0:T(8,128)(2,1)} %get-tuple-element.4) | copy-start | bytes 1966084
  89.3 38.1 %all-to-all-start.1 = ((bf16[1,128,2,1280]{3,2,0,1:T(2,128)(2,1)}), bf16[1,128,2,1280]{3,2,0,1:T(2,128)(2,1)S(1)}, u32[]{:S(2)}, u32[]{:S(2)}) async-start(bf16[1,128,2,1280]{3,2,0,1:T(2,128)(2,1)} %copy.14), calls=%async_computation.1 | async-start | bytes 1310720 | tf_op jit(solution)/shard_map/all_to_all | solution.py:16
  127.4 29.2 %all-to-all-start = ((bf16[1,128,2,1280]{3,2,0,1:T(2,128)(2,1)}), bf16[1,128,2,1280]{3,2,0,1:T(2,128)(2,1)S(1)}, u32[]{:S(2)}, u32[]{:S(2)}) async-start(bf16[1,128,2,1280]{3,2,0,1:T(2,128)(2,1)} %copy.13), calls=%async_computation | async-start | bytes 1310720 | tf_op jit(solution)/shard_map/all_to_all | solution.py:16
  135.7 81.7 %all-reduce.9.cloned.1.call-start = ((), (), s32[]{:S(2)}) async-start(), calls=%async_computation.5 | async-start | bytes 2621440 | tf_op jit(solution)/shard_map/psum | solution.py:22
  160.0 4.5 copy-start.2
  217.3 19.2 %copy-start.5 = (bf16[1,128,2,1280]{3,1,2,0:T(8,128)(2,1)S(1)}, bf16[1,128,2,1280]{3,1,2,0:T(8,128)(2,1)}, u32[]{:S(2)}) copy-start(bf16[1,128,2,1280]{3,1,2,0:T(8,128)(2,1)} %get-tuple-element.3) | copy-start | bytes 1966084
  220.0 38.3 %all-to-all-start.2 = ((bf16[1,128,2,1280]{3,2,0,1:T(2,128)(2,1)}), bf16[1,128,2,1280]{3,2,0,1:T(2,128)(2,1)S(1)}, u32[]{:S(2)}, u32[]{:S(2)}) async-start(bf16[1,128,2,1280]{3,2,0,1:T(2,128)(2,1)} %copy.16), calls=%async_computation.2 | async-start | bytes 1310720 | tf_op jit(solution)/shard_map/all_to_all | solution.py:23
  236.5 30.1 %copy-start.1 = (bf16[2,64,1280]{2,1,0:T(8,128)(2,1)S(1)}, bf16[2,64,1280]{2,1,0:T(8,128)(2,1)}, u32[]{:S(2)}) copy-start(bf16[2,64,1280]{2,1,0:T(8,128)(2,1)} %param.5) | copy-start | bytes 983044
  258.3 29.1 %all-to-all-start.3 = ((bf16[1,128,2,1280]{3,2,0,1:T(2,128)(2,1)}), bf16[1,128,2,1280]{3,2,0,1:T(2,128)(2,1)S(1)}, u32[]{:S(2)}, u32[]{:S(2)}) async-start(bf16[1,128,2,1280]{3,2,0,1:T(2,128)(2,1)} %copy.19), calls=%async_computation.3 | async-start | bytes 1310720 | tf_op jit(solution)/shard_map/all_to_all | solution.py:23
  266.6 289.3 %all-reduce.7.cloned.1.call-start = ((), (), s32[]{:S(2)}) async-start(), calls=%async_computation.4 | async-start | bytes 1310720
  290.2 1.0 copy-start.3
Sparse Core Ops, SparseCore 0:
  30.6 55.9 all-reduce.10
  167.1 50.2 all-reduce.8
  290.3 265.5 all-reduce.6
where the time goes:
time: 565 us; the launch traced here: 564 us
  waiting for transfers between devices  440 us (78%)
  starting transfers between devices  49.5 us (9%)
  blocking collectives  24.2 us (4%)
  matrix products  20 us (4%)
  local copies, waits for them, and re-layouts  15.4 us (3%)
  between operations  13.9 us (2%)
    unnamed x4, waiting for transfers between devices  264 us
    psum x1, waiting for transfers between devices, to_experts(): summed = lax.psum(parts.astype(jnp.bfloat16), 'hidden')  56.2 us
    psum x1, waiting for transfers between devices, from_experts(): summed = lax.psum(stacked.astype(jnp.bfloat16), 'hidden')  50.4 us
    all_to_all x2, waiting for transfers between devices, to_experts(): lax.all_to_all(summed, 'expert', split_axis=1, concat_axis=2, tiled=True)  36.1 us
    all_to_all x2, waiting for transfers between devices, from_experts(): lax.all_to_all(summed, 'expert', split_axis=1, concat_axis=1, tiled=True)  34.2 us
    all_to_all x2, starting transfers between devices, from_experts(): lax.all_to_all(summed, 'expert', split_axis=1, concat_axis=1, tiled=True)  24.8 us
    all_to_all x2, starting transfers between devices, to_experts(): lax.all_to_all(summed, 'expert', split_axis=1, concat_axis=2, tiled=True)  24.6 us
    pmax x1, blocking collectives, shards(): column_top = lax.pmax(jnp.max(logits, axis=1), 'hidden')  11.9 us
  transfers between devices with their start and end apart: 7, of which 7 were waited for; matrix products, arithmetic and copies ran while one was open for 2% of the time, Pallas kernels for 0%

commit v1 on v0

v1 whole, which is shorter than its diff:
```python
import functools

import jax
import jax.numpy as jnp
from jax import lax
from jax.experimental import pallas as pl
from jax.experimental.pallas import tpu as pltpu
from jax.sharding import PartitionSpec as P

half_root = 0.7071067811865476
density_scale = 0.3989422804014327
MESH = pl.DeviceIdType.MESH
f32 = jnp.float32
bf16 = jnp.bfloat16
NT = (((1,), (1,)), ((), ()))
TN = (((0,), (0,)), ((), ()))
NN = (((1,), (0,)), ((), ()))


def mm(a, b, dims=NN):
    return lax.dot_general(a, b, dims, preferred_element_type=f32)


def gelu_parts(pre):
    cdf = 0.5 * (1.0 + lax.erf(pre * half_root))
    return pre * cdf, cdf + pre * jnp.exp(-0.5 * pre * pre) * density_scale


def kernel(
    n, stride, tok_hbm, emb_hbm, win_hbm, wout_hbm, go_hbm, gt_out, ge_out,
    tok_v, emb_v, win_v, wout_v, lg_own, lg, tok_d, go_d, tok_o,
    disp_v, comb_v, send_f, rows_f, d_own, d_core, d_chip, d_diag,
    po_send, po_recv, acc, xs_send, xs_recv, send_b, rows_b,
    gl_send, gl_recv, gt_send, ef, send_e, recv_e, fin, lsem, ssem, rsem, wsem,
):
    g = lax.axis_index("expert")
    h = lax.axis_index("hidden")
    j = h // 2
    k = h % 2
    half = tok_d.shape[2]
    tk = tok_d.shape[1]
    others = [(j, 1 - k), (1 - j, k), (1 - j, 1 - k)]

    def device(where):
        return (g, 2 * where[0] + where[1])

    def cols(core):
        return pl.ds(pl.multiple_of(core * half, 128), half)

    def remote(src, dst, s, r, where):
        return pltpu.make_async_remote_copy(
            src_ref=src, dst_ref=dst, send_sem=ssem.at[s], recv_sem=rsem.at[r],
            device_id=device(where), device_id_type=MESH,
        )

    def partner(s):
        t = lax.rem(g + lax.rem(s * stride, n), n)
        odd = lax.rem(s, 2)
        return t, 2 * (j + odd - 2 * j * odd) + k

    loads = [
        pltpu.make_async_copy(tok_hbm, tok_v, lsem.at[0]),
        pltpu.make_async_copy(emb_hbm, emb_v, lsem.at[1]),
        pltpu.make_async_copy(win_hbm.at[0], win_v, lsem.at[2]),
        pltpu.make_async_copy(wout_hbm.at[0], wout_v, lsem.at[3]),
        pltpu.make_async_copy(tok_hbm.at[j, :, cols(k)], tok_d.at[h], lsem.at[4]),
        pltpu.make_async_copy(go_hbm.at[j, :, cols(k)], go_d.at[h], lsem.at[5]),
    ]
    for load in loads:
        load.start()

    barrier = pltpu.get_barrier_semaphore()
    for where in others:
        pl.semaphore_signal(barrier, inc=1, device_id=device(where), device_id_type=MESH)

    def greet(s, carry):
        pl.semaphore_signal(barrier, inc=1, device_id=partner(s), device_id_type=MESH)
        return carry

    lax.fori_loop(1, n, greet, 0)

    loads[0].wait()
    loads[1].wait()
    for image in range(2):
        lg_own[image] = mm(tok_v[image], emb_v[...], NT)
    lg[h] = lg_own[j]
    pl.semaphore_wait(barrier, n + 2)

    tok_c, lg_c, go_c = [], [], []
    for i in (1, 2, 0):
        where = others[i]
        copy = remote(lg_own.at[where[0]], lg.at[h], i, i, where)
        copy.start()
        lg_c.append(copy)
    for i in (1, 2, 0):
        where = others[i]
        copy = remote(tok_hbm.at[where[0], :, cols(where[1])], tok_d.at[h], 3 + i, 3 + i, where)
        copy.start()
        tok_c.append(copy)
    for i in (1, 2, 0):
        where = others[i]
        copy = remote(go_hbm.at[where[0], :, cols(where[1])], go_d.at[h], 6 + i, 6 + i, where)
        copy.start()
        go_c.append(copy)

    for copy in lg_c:
        copy.wait_recv()
    logits = lg[...].reshape(4 * tk, n)
    col = jnp.exp(logits - jnp.max(logits, axis=0, keepdims=True))
    disp = col / jnp.sum(col, axis=0, keepdims=True)
    row = jnp.exp(logits - jnp.max(logits, axis=1, keepdims=True))
    comb = row / jnp.sum(row, axis=1, keepdims=True)
    disp_v[...] = disp
    comb_v[...] = comb

    for copy in tok_c:
        copy.wait_recv()
    loads[4].wait()
    tok_x = remote(tok_d, tok_o, 9, 9, others[0])
    tok_x.start()
    slot_rows = mm(disp.astype(bf16), tok_d[...].reshape(4 * tk, half), TN).astype(bf16)
    for copy in go_c:
        copy.wait_recv()
    loads[5].wait()
    grad_rows = mm(comb.astype(bf16), go_d[...].reshape(4 * tk, half), TN).astype(bf16)
    send_f[...] = jnp.stack([slot_rows, grad_rows], axis=1)

    def spread(src, dst, sem):
        own = pltpu.make_async_copy(src.at[g], dst.at[g], lsem.at[6 + sem])
        own.start()

        def step(s, carry):
            t, at = partner(s)
            pltpu.make_async_remote_copy(
                src_ref=src.at[t], dst_ref=dst.at[g], send_sem=wsem.at[2 * sem],
                recv_sem=wsem.at[2 * sem + 1], device_id=(t, at), device_id_type=MESH,
            ).start()
            return carry

        lax.fori_loop(1, n, step, 0)
        return own

    def wait_all(ref, count, sem):
        part = ref.at[pl.ds(0, count)]
        pltpu.make_async_copy(part, part, sem).wait()

    own_f = spread(send_f, rows_f, 0)
    own_f.wait()
    wait_all(rows_f, n - 1, wsem.at[1])
    loads[2].wait()
    loads[3].wait()

    d_own[0] = rows_f[:, 0, :]
    d_own[1] = rows_f[:, 1, :]
    to_chip = remote(d_own, d_chip, 10, 10, others[1])
    to_chip.start()
    to_core = remote(d_own, d_core, 11, 11, others[0])
    to_core.start()

    def expert(mine, other, index):
        mine_at = pl.ds(pl.multiple_of(k * half, 128), half)
        other_at = pl.ds(pl.multiple_of((1 - k) * half, 128), half)
        pre = mm(mine[0], win_v[mine_at, :]) + mm(other[0], win_v[other_at, :])
        ga = mm(mine[1], wout_v[:, mine_at], NT) + mm(other[1], wout_v[:, other_at], NT)
        act, slope = gelu_parts(pre)
        act = act.astype(bf16)
        gp = (ga * slope).astype(bf16)
        po_send[index, 0] = mm(act, wout_v[:, other_at]).astype(bf16)
        po_send[index, 1] = mm(gp, win_v[other_at, :], NT).astype(bf16)
        give = remote(po_send.at[index], po_recv.at[index], 13 + index, 13 + index, others[0])
        give.start()
        acc[index, 0] = mm(act, wout_v[:, mine_at])
        acc[index, 1] = mm(gp, win_v[mine_at, :], NT)
        return give

    to_core.wait_recv()
    give0 = expert(d_own, d_core, 0)
    to_chip.wait_recv()
    forward = remote(d_chip, d_diag, 12, 12, others[0])
    forward.start()
    forward.wait_recv()
    give1 = expert(d_chip, d_diag, 1)
    give1.wait_recv()
    xs_send[...] = (acc[1] + po_recv[1].astype(f32)).astype(bf16)
    cross = remote(xs_send, xs_recv, 15, 15, others[1])
    cross.start()
    give0.wait_recv()
    total = acc[0] + po_recv[0].astype(f32)
    cross.wait_recv()
    total = (total + xs_recv[...].astype(f32)).astype(bf16)
    send_b[...] = jnp.stack([total[0], total[1]], axis=1)

    own_b = spread(send_b, rows_b, 1)
    own_b.wait()
    wait_all(rows_b, n - 1, wsem.at[3])

    slot_out = rows_b[:, 0, :]
    slot_grad = rows_b[:, 1, :]
    tok2 = tok_d[...].reshape(4 * tk, half)
    go2 = go_d[...].reshape(4 * tk, half)
    disp = disp_v[...]
    comb = comb_v[...]
    gc = comb * mm(go2, slot_out, NT)
    gd = disp * mm(tok2, slot_grad, NT)
    gl = gc - comb * jnp.sum(gc, axis=1, keepdims=True)
    gl = gl + gd - disp * jnp.sum(gd, axis=0, keepdims=True)
    gl_send[...] = gl
    gl_x = remote(gl_send, gl_recv, 16, 16, others[0])
    gl_x.start()
    first = mm(disp.astype(bf16), slot_grad)
    tok_x.wait_recv()
    gl_x.wait_recv()
    gl = (gl_send[...] + gl_recv[...]).astype(bf16)

    ef[k] = mm(gl, tok2, TN)
    ef[1 - k] = mm(gl, tok_o[...].reshape(4 * tk, half), TN)
    hn = n // 2
    mine = pl.ds(pl.multiple_of(k * hn, hn), hn)
    send_e[...] = jnp.stack([ef[0, mine, :].astype(bf16), ef[1, mine, :].astype(bf16)], axis=1)
    keeper = k == g // hn
    own_e = pltpu.make_async_copy(send_e.at[lax.rem(g, hn)], recv_e.at[g], lsem.at[8])

    def send_piece(s):
        e = lax.rem(g + lax.rem(s * stride, hn), hn)
        t = k * hn + e
        odd = lax.rem(s, 2)
        pltpu.make_async_remote_copy(
            src_ref=send_e.at[e], dst_ref=recv_e.at[g], send_sem=wsem.at[4],
            recv_sem=wsem.at[5], device_id=(t, 2 * (j + odd - 2 * j * odd) + k),
            device_id_type=MESH,
        ).start()

    def piece(s, carry):
        send_piece(s)
        return carry

    lax.fori_loop(1, hn, piece, 0)

    @pl.when(keeper)
    def _():
        own_e.start()

    @pl.when(jnp.logical_not(keeper))
    def _():
        send_piece(0)

    second = mm(gl, emb_v[:, cols(k)])
    gt_send[...] = (first + second).astype(bf16).reshape(4, tk, half)
    own_t = pltpu.make_async_copy(gt_send.at[h], gt_out.at[j, :, cols(k)], lsem.at[9])
    own_t.start()
    gt_c = []
    for i in (1, 2, 0):
        where = others[i]
        copy = remote(
            gt_send.at[2 * where[0] + where[1]], gt_out.at[j, :, cols(k)], 17 + i, 17 + i, where
        )
        copy.start()
        gt_c.append(copy)

    fin_c = [remote(fin.at[j], fin.at[j], 20 + i, 23 + j, others[i]) for i in range(3)]

    @pl.when(keeper)
    def _():
        own_e.wait()
        wait_all(recv_e, n - 1, wsem.at[5])
        rows = recv_e[...].reshape(2 * n, half)
        shape = (8, 2 * n)
        pick = lax.rem(lax.broadcasted_iota(jnp.int32, shape, 1), 2)
        pick = (pick == lax.broadcasted_iota(jnp.int32, shape, 0)).astype(bf16)
        fin[j] = mm(pick, rows)[0:2, :]
        for copy in fin_c:
            copy.start()
        for copy in fin_c:
            copy.wait_send()
        wait_all(send_e, hn - 1, wsem.at[4])
        pltpu.make_async_copy(fin.at[1 - j], fin.at[1 - j], rsem.at[24 - j]).wait()

    @pl.when(jnp.logical_not(keeper))
    def _():
        wait_all(send_e, hn, wsem.at[4])
        for chip in range(2):
            pltpu.make_async_copy(fin.at[chip], fin.at[chip], rsem.at[23 + chip]).wait()

    both = fin[0] + fin[1]
    row = jnp.where(j == 0, both[0:1, :], both[1:2, :])
    quarter = half // 2
    ge_out[...] = jnp.where(k == 0, row[:, :quarter], row[:, quarter:])

    own_t.wait()
    for copy in gt_c:
        copy.wait_recv()
    for copy in lg_c + tok_c + go_c + gt_c + [
        tok_x, to_chip, to_core, give0, give1, forward, cross, gl_x
    ]:
        copy.wait_send()
    wait_all(send_f, n - 1, wsem.at[0])
    wait_all(send_b, n - 1, wsem.at[2])


def shards(n, tokens, slot_embed, w_in, w_out, grad_out):
    images, tk, width = tokens.shape
    ff = w_in.shape[2]
    half = width // 2
    hbm = pl.BlockSpec(memory_space=pl.ANY)
    vm = pltpu.VMEM
    scratch = [
        vm((images, tk, width), bf16), vm((n, width), bf16), vm((width, ff), bf16),
        vm((ff, width), bf16), vm((images, tk, n), f32), vm((4, tk, n), f32),
        vm((4, tk, half), bf16), vm((4, tk, half), bf16), vm((4, tk, half), bf16),
        vm((4 * tk, n), f32), vm((4 * tk, n), f32),
        vm((n, 2, half), bf16), vm((n, 2, half), bf16),
        vm((2, n, half), bf16), vm((2, n, half), bf16), vm((2, n, half), bf16),
        vm((2, n, half), bf16),
        vm((2, 2, n, half), bf16), vm((2, 2, n, half), bf16), vm((2, 2, n, half), f32),
        vm((2, n, half), bf16), vm((2, n, half), bf16),
        vm((n, 2, half), bf16), vm((n, 2, half), bf16),
        vm((4 * tk, n), f32), vm((4 * tk, n), f32), vm((4, tk, half), bf16),
        vm((2, n, half), f32), vm((n // 2, 2, half), bf16), vm((n, 2, half), bf16),
        vm((2, 2, half), f32),
        pltpu.SemaphoreType.DMA((10,)), pltpu.SemaphoreType.DMA((25,)),
        pltpu.SemaphoreType.DMA((25,)), pltpu.SemaphoreType.DMA((6,)),
    ]
    stride = 37 if n == 128 else 1
    return pl.pallas_call(
        functools.partial(kernel, n, stride),
        out_shape=(
            jax.ShapeDtypeStruct(tokens.shape, bf16),
            jax.ShapeDtypeStruct((1, width // 4), f32),
        ),
        in_specs=[hbm] * 5,
        out_specs=(hbm, pl.BlockSpec(memory_space=pltpu.VMEM)),
        scratch_shapes=scratch,
        compiler_params=pltpu.CompilerParams(
            collective_id=0, has_side_effects=True, vmem_limit_bytes=40 * 2**20
        ),
        cost_estimate=pl.CostEstimate(
            flops=2 * 10**9, bytes_accessed=6 * 10**6, transcendentals=10**6
        ),
    )(tokens, slot_embed, w_in, w_out, grad_out)


def solution(mesh):
    return jax.shard_map(
        functools.partial(shards, mesh.shape["expert"]),
        mesh=mesh,
        in_specs=(
            P("expert", "hidden", None),
            P(),
            P("expert", None, "hidden"),
            P("expert", "hidden", None),
            P("expert", "hidden", None),
        ),
        out_specs=(P("expert", "hidden", None), P("expert", "hidden")),
        check_vma=False,
    )
```

time: 565 us -> 102 us (0.18)
  waiting for transfers between devices: 440 us -> 0 us
  Pallas kernels: 0 us -> 93.7 us
  starting transfers between devices: 49.5 us -> 0 us
  blocking collectives: 24.2 us -> 0 us
  matrix products: 20 us -> 0 us
  between operations: 13.9 us -> 0.65 us
  local copies, waits for them, and re-layouts: 15.4 us -> 7.06 us
    unnamed x4 -> x0, waiting for transfers between devices: 264 us -> none
    psum x2 -> x0, waiting for transfers between devices: 107 us -> none  [the longest x1 56.2 us: to_experts(): summed = lax.psum(parts.astype(jnp.bfloat16), 'hidden')]
    pallas_call x0 -> x1, Pallas kernels: none -> 93.7 us  [shards(): pl.pallas_call(functools.partial(kernel, n, stride), out_shape=(jax.Shape...]
    all_to_all x4 -> x0, waiting for transfers between devices: 70.3 us -> none  [the longest x2 36.1 us: to_experts(): lax.all_to_all(summed, 'expert', split_axis=1, concat_axis=2, tiled=True)]
    all_to_all x4 -> x0, starting transfers between devices: 49.3 us -> none  [the longest x2 24.8 us: from_experts(): lax.all_to_all(summed, 'expert', split_axis=1, concat_axis=1, tiled=True)]
    dot_general x12 -> x0, matrix products: 20 us -> none  [the longest x1 3.88 us: expert_forward(): pre = jnp.dot(rows, w_in[0], preferred_element_type=jnp.float32)]
    psum x2 -> x0, blocking collectives: 12.3 us -> none  [the longest x1 6.53 us: shards(): disp_inner = lax.psum(jnp.sum(dispatch * grad_disp, axis=1), 'hidden')]
    pmax x1 -> x0, blocking collectives: 11.9 us -> none  [shards(): column_top = lax.pmax(jnp.max(logits, axis=1), 'hidden')]
  transfers between devices with their start and end apart: 7 -> 0, of which waited for: 7 -> 0; matrix products, arithmetic and copies ran while one was open for 2% -> 0% of each run, Pallas kernels for 0% -> 0%
where the time goes in v1:
time: 102 us; the launch traced here: 101 us
  Pallas kernels  93.7 us (92%)
  local copies, waits for them, and re-layouts  7.06 us (7%)
    pallas_call x1, Pallas kernels, shards(): pl.pallas_call(functools.partial(kernel, n, stride), out_shape=(jax.Shape...  93.7 us
    unnamed x12, local copies, waits for them, and re-layouts  7.06 us

profile of v1, /device:TPU:1, one launch (start us, length us, event | category | flops | bytes accessed | tf_op | source)
XLA Modules:
  0.0 101.4 jit_solution(3647559277783011939)
XLA Ops:
  0.6 0.0 copy-start
  0.6 1.4 %copy-done = bf16[1,1280,640]{2,1,0:T(8,128)(2,1)S(1)} copy-done((bf16[1,1280,640]{2,1,0:T(8,128)(2,1)S(1)}, bf16[1,1280,640]{2,1,0:T(8,128)(2,1)}, u32[]{:S(2)}) %copy-start) | copy-done | bytes 1638424
  2.1 0.0 copy-start.1
  2.1 1.4 %copy-done.1 = bf16[1,640,1280]{2,1,0:T(8,128)(2,1)S(1)} copy-done((bf16[1,640,1280]{2,1,0:T(8,128)(2,1)S(1)}, bf16[1,640,1280]{2,1,0:T(8,128)(2,1)}, u32[]{:S(2)}) %copy-start.1) | copy-done | bytes 1638424
  3.5 0.0 copy-start.2
  3.5 1.0 copy-done.2
  4.5 0.0 copy-start.3
  4.5 1.0 copy-done.3
  5.4 0.0 copy-start.4
  5.4 1.0 copy-done.4
  6.4 93.7 %shard_map.68 = (bf16[2,64,1280]{2,1,0:T(8,128)(2,1)S(1)}, f32[1,320]{1,0:T(1,128)S(1)}) custom-call(bf16[2,64,1280]{2,1,0:T(8,128)(2,1)S(1)} %copy-done.2, bf16[128,1280]{1,0:T(8,128)(2,1)S(1)} %copy-done.3, bf16[1,1280,640]{2,1,0:T(8,128)(2,1)S(1)} %copy-done, bf16[1,640,1280]{2,1,0:T(8,128)(2,1)S(1)} %copy-done.1, bf16[2,64,1280]{2,1,0:T(8,128)(2,1)S(1)} %copy-done.4), custom_call_target="tpu_custom_call" | custom-call | flops 2000000000 | bytes 6000000 | tf_op jit(solution)/shard_map/pallas_call | solution.py:324
  100.2 0.7 copy.9
  100.9 0.6 copy.10
Async XLA Ops:
  0.6 1.4 %copy-start = (bf16[1,1280,640]{2,1,0:T(8,128)(2,1)S(1)}, bf16[1,1280,640]{2,1,0:T(8,128)(2,1)}, u32[]{:S(2)}) copy-start(bf16[1,1280,640]{2,1,0:T(8,128)(2,1)} %win_hbm.1) | copy-start | bytes 4915204
  2.1 1.4 %copy-start.1 = (bf16[1,640,1280]{2,1,0:T(8,128)(2,1)S(1)}, bf16[1,640,1280]{2,1,0:T(8,128)(2,1)}, u32[]{:S(2)}) copy-start(bf16[1,640,1280]{2,1,0:T(8,128)(2,1)} %wout_hbm.1) | copy-start | bytes 4915204
  3.5 1.0 copy-start.2
  4.5 1.0 copy-start.3
  5.4 1.0 copy-start.4

commit v2 on v1

--- a/solution.py
+++ b/solution.py
@@ -27,11 +27,11 @@
 
 
 def kernel(
-    n, stride, tok_hbm, emb_hbm, win_hbm, wout_hbm, go_hbm, gt_out, ge_out,
+    n, nz, stride, tok_hbm, emb_hbm, win_hbm, wout_hbm, go_hbm, gt_out, ge_out,
     tok_v, emb_v, win_v, wout_v, lg_own, lg, tok_d, go_d, tok_o,
     disp_v, comb_v, send_f, rows_f, d_own, d_core, d_chip, d_diag,
     po_send, po_recv, acc, xs_send, xs_recv, send_b, rows_b,
-    gl_send, gl_recv, gt_send, ef, send_e, recv_e, fin, lsem, ssem, rsem, wsem,
+    gl_send, gl_recv, gt_send, ef, send_e, recv_e, fin, lsem, ssem, rsem, wsem, here,
 ):
     g = lax.axis_index("expert")
     h = lax.axis_index("hidden")
@@ -69,22 +69,31 @@
     for load in loads:
         load.start()
 
+    zy = n // 2
+    ny = zy // nz
+    a = g % 2
+    z = (g // 2) % nz
+    y = g // (2 * nz)
+    along_z = [((y * nz + (z + i) % nz) * 2 + a, h) for i in range(1, nz)]
+    along_y = [((((y + i) % ny) * nz + z) * 2 + a, h) for i in range(1, ny)]
+    along_x = (g + 1 - 2 * a, 2 * (1 - j) + k)
+
+    def tell(semaphore, peer):
+        pl.semaphore_signal(semaphore, inc=1, device_id=peer, device_id_type=MESH)
+
     barrier = pltpu.get_barrier_semaphore()
-    for where in others:
-        pl.semaphore_signal(barrier, inc=1, device_id=device(where), device_id_type=MESH)
-
-    def greet(s, carry):
-        pl.semaphore_signal(barrier, inc=1, device_id=partner(s), device_id_type=MESH)
-        return carry
-
-    lax.fori_loop(1, n, greet, 0)
+    direct = [device(where) for where in others] + along_y + along_z + [along_x]
+    for peer in direct:
+        tell(barrier, peer)
 
     loads[0].wait()
     loads[1].wait()
     for image in range(2):
         lg_own[image] = mm(tok_v[image], emb_v[...], NT)
     lg[h] = lg_own[j]
-    pl.semaphore_wait(barrier, n + 2)
+    pl.semaphore_wait(barrier, len(direct))
+    for peer in along_z:
+        tell(here.at[0], peer)
 
     tok_c, lg_c, go_c = [], [], []
     for i in (1, 2, 0):
@@ -124,6 +133,11 @@
     loads[5].wait()
     grad_rows = mm(comb.astype(bf16), go_d[...].reshape(4 * tk, half), TN).astype(bf16)
     send_f[...] = jnp.stack([slot_rows, grad_rows], axis=1)
+
+    if nz > 1:
+        pl.semaphore_wait(here.at[0], nz - 1)
+    tell(here.at[1], along_x)
+    pl.semaphore_wait(here.at[1], 1)
 
     def spread(src, dst, sem):
         own = pltpu.make_async_copy(src.at[g], dst.at[g], lsem.at[6 + sem])
@@ -301,7 +315,7 @@
     images, tk, width = tokens.shape
     ff = w_in.shape[2]
     half = width // 2
-    hbm = pl.BlockSpec(memory_space=pl.ANY)
+    hbm = pl.BlockSpec(memory_space=pltpu.HBM)
     vm = pltpu.VMEM
     scratch = [
         vm((images, tk, width), bf16), vm((n, width), bf16), vm((width, ff), bf16),
@@ -319,10 +333,12 @@
         vm((2, 2, half), f32),
         pltpu.SemaphoreType.DMA((10,)), pltpu.SemaphoreType.DMA((25,)),
         pltpu.SemaphoreType.DMA((25,)), pltpu.SemaphoreType.DMA((6,)),
+        pltpu.SemaphoreType.REGULAR((2,)),
     ]
     stride = 37 if n == 128 else 1
+    nz = 8 if n == 128 else 2
     return pl.pallas_call(
-        functools.partial(kernel, n, stride),
+        functools.partial(kernel, n, nz, stride),
         out_shape=(
             jax.ShapeDtypeStruct(tokens.shape, bf16),
             jax.ShapeDtypeStruct((1, width // 4), f32),
@@ -331,7 +347,7 @@
         out_specs=(hbm, pl.BlockSpec(memory_space=pltpu.VMEM)),
         scratch_shapes=scratch,
         compiler_params=pltpu.CompilerParams(
-            collective_id=0, has_side_effects=True, vmem_limit_bytes=40 * 2**20
+            collective_id=0, has_side_effects=True, vmem_limit_bytes=60 * 2**20
         ),
         cost_estimate=pl.CostEstimate(
             flops=2 * 10**9, bytes_accessed=6 * 10**6, transcendentals=10**6

time: 102 us -> 93.6 us (0.918)
  local copies, waits for them, and re-layouts: 7.06 us -> 2.96 us
  Pallas kernels: 93.7 us -> 89.8 us
    unnamed x12 -> x2, local copies, waits for them, and re-layouts: 7.06 us -> 2.96 us
    pallas_call x1, Pallas kernels: 93.7 us -> 89.8 us  [shards(): pl.pallas_call(functools.partial(kernel, n, nz, stride), out_shape=(jax.S...]
where the time goes in v2:
time: 93.6 us; the launch traced here: 93.4 us
  Pallas kernels  89.8 us (96%)
  local copies, waits for them, and re-layouts  2.96 us (3%)
    pallas_call x1, Pallas kernels, shards(): pl.pallas_call(functools.partial(kernel, n, nz, stride), out_shape=(jax.S...  89.8 us
    unnamed x2, local copies, waits for them, and re-layouts  2.96 us

profile of v2, /device:TPU:1, one launch (start us, length us, event | category | flops | bytes accessed | tf_op | source)
XLA Modules:
  0.0 93.4 jit_solution(44835151305897)
XLA Ops:
  0.6 89.8 %shard_map.68 = (bf16[2,64,1280]{2,1,0:T(8,128)(2,1)}, f32[1,320]{1,0:T(1,128)}) custom-call(bf16[2,64,1280]{2,1,0:T(8,128)(2,1)} %tok_hbm.1, bf16[128,1280]{1,0:T(8,128)(2,1)} %emb_hbm.1, bf16[1,1280,640]{2,1,0:T(8,128)(2,1)} %win_hbm.1, bf16[1,640,1280]{2,1,0:T(8,128)(2,1)} %wout_hbm.1, bf16[2,64,1280]{2,1,0:T(8,128)(2,1)} %go_hbm.1), custom_call_target="tpu_custom_call" | custom-call | flops 2000000000 | bytes 6000000 | tf_op jit(solution)/shard_map/pallas_call | solution.py:340
  90.4 1.7 %copy.9 = bf16[2,64,1280]{2,1,0:T(8,128)(2,1)} copy(bf16[2,64,1280]{2,1,0:T(8,128)(2,1)} %get-tuple-element.4) | data formatting | bytes 655360
  92.1 1.2 %copy.10 = f32[1,320]{1,0:T(1,128)} copy(f32[1,320]{1,0:T(1,128)} %get-tuple-element.5) | data formatting | bytes 2560

commit v3 on v2

--- a/solution.py
+++ b/solution.py
@@ -29,9 +29,9 @@
 def kernel(
     n, nz, stride, tok_hbm, emb_hbm, win_hbm, wout_hbm, go_hbm, gt_out, ge_out,
     tok_v, emb_v, win_v, wout_v, lg_own, lg, tok_d, go_d, tok_o,
-    disp_v, comb_v, send_f, rows_f, d_own, d_core, d_chip, d_diag,
+    disp_v, comb_v, send_f, rows_f, mine, other, win_t, wout_t,
     po_send, po_recv, acc, xs_send, xs_recv, send_b, rows_b,
-    gl_send, gl_recv, gt_send, ef, send_e, recv_e, fin, lsem, ssem, rsem, wsem, here,
+    gl_send, gl_recv, gt_send, ef, send_e, recv_e, fin, lsem, ssem, rsem, wsem, fsem, here,
 ):
     g = lax.axis_index("expert")
     h = lax.axis_index("hidden")
@@ -91,6 +91,10 @@
     for image in range(2):
         lg_own[image] = mm(tok_v[image], emb_v[...], NT)
     lg[h] = lg_own[j]
+    loads[2].wait()
+    win_t[...] = win_v[...].T
+    loads[3].wait()
+    wout_t[...] = wout_v[...].T
     pl.semaphore_wait(barrier, len(direct))
     for peer in along_z:
         tell(here.at[0], peer)
@@ -139,72 +143,109 @@
     tell(here.at[1], along_x)
     pl.semaphore_wait(here.at[1], 1)
 
-    def spread(src, dst, sem):
-        own = pltpu.make_async_copy(src.at[g], dst.at[g], lsem.at[6 + sem])
-        own.start()
-
+    def wait_all(ref, count, sem):
+        part = ref.at[pl.ds(0, count)]
+        pltpu.make_async_copy(part, part, sem).wait()
+
+    chunks = mine.shape[0]
+    size = n // chunks
+    mine_at = cols(k)
+    other_at = cols(1 - k)
+
+    def piece(chunk):
+        return pl.ds(chunk * size, size)
+
+    own_f = pltpu.make_async_copy(send_f.at[g], rows_f.at[0], lsem.at[6])
+    own_f.start()
+    own_b = pltpu.make_async_copy(send_b.at[0], rows_b.at[g], lsem.at[7])
+
+    def out_chunk(chunk):
         def step(s, carry):
             t, at = partner(s)
             pltpu.make_async_remote_copy(
-                src_ref=src.at[t], dst_ref=dst.at[g], send_sem=wsem.at[2 * sem],
-                recv_sem=wsem.at[2 * sem + 1], device_id=(t, at), device_id_type=MESH,
+                src_ref=send_f.at[t], dst_ref=rows_f.at[s], send_sem=wsem.at[0],
+                recv_sem=fsem.at[chunk], device_id=(t, at), device_id_type=MESH,
             ).start()
             return carry
 
-        lax.fori_loop(1, n, step, 0)
-        return own
-
-    def wait_all(ref, count, sem):
-        part = ref.at[pl.ds(0, count)]
-        pltpu.make_async_copy(part, part, sem).wait()
-
-    own_f = spread(send_f, rows_f, 0)
-    own_f.wait()
-    wait_all(rows_f, n - 1, wsem.at[1])
-    loads[2].wait()
-    loads[3].wait()
-
-    d_own[0] = rows_f[:, 0, :]
-    d_own[1] = rows_f[:, 1, :]
-    to_chip = remote(d_own, d_chip, 10, 10, others[1])
-    to_chip.start()
-    to_core = remote(d_own, d_core, 11, 11, others[0])
-    to_core.start()
-
-    def expert(mine, other, index):
-        mine_at = pl.ds(pl.multiple_of(k * half, 128), half)
-        other_at = pl.ds(pl.multiple_of((1 - k) * half, 128), half)
-        pre = mm(mine[0], win_v[mine_at, :]) + mm(other[0], win_v[other_at, :])
-        ga = mm(mine[1], wout_v[:, mine_at], NT) + mm(other[1], wout_v[:, other_at], NT)
+        lax.fori_loop(max(chunk * size, 1), (chunk + 1) * size, step, 0)
+
+    def back_chunk(chunk):
+        def step(s, carry):
+            t, at = partner(n - s)
+            pltpu.make_async_remote_copy(
+                src_ref=send_b.at[s], dst_ref=rows_b.at[g], send_sem=wsem.at[2],
+                recv_sem=wsem.at[3], device_id=(t, at), device_id_type=MESH,
+            ).start()
+            return carry
+
+        lax.fori_loop(max(chunk * size, 1), (chunk + 1) * size, step, 0)
+
+    to_chip = [
+        remote(mine.at[c, :, 0], mine.at[c, :, 1], 30 + c, 30 + c, others[1]) for c in range(chunks)
+    ]
+    to_core = [
+        remote(mine.at[c], other.at[c], 40 + c, 40 + c, others[0]) for c in range(chunks)
+    ]
+    give = [
+        remote(po_send.at[c], po_recv.at[c], 50 + c, 50 + c, others[0]) for c in range(chunks)
+    ]
+    cross = [
+        remote(xs_send.at[c], xs_recv.at[c], 60 + c, 60 + c, others[1]) for c in range(chunks)
+    ]
+
+    def arrive(c):
+        if c == 0:
+            own_f.wait()
+        wait_all(rows_f, size - (c == 0), fsem.at[c])
+        mine[c, 0, 0] = rows_f[piece(c), 0, :]
+        mine[c, 1, 0] = rows_f[piece(c), 1, :]
+        to_chip[c].start()
+
+    def share(c):
+        to_chip[c].wait_recv()
+        to_core[c].start()
+
+    def expert(c):
+        to_core[c].wait_recv()
+        mine0 = mine[c, 0].reshape(2 * size, half)
+        mine1 = mine[c, 1].reshape(2 * size, half)
+        other0 = other[c, 0].reshape(2 * size, half)
+        other1 = other[c, 1].reshape(2 * size, half)
+        pre = mm(mine0, win_v[mine_at, :]) + mm(other0, win_v[other_at, :])
+        ga = mm(mine1, wout_t[mine_at, :]) + mm(other1, wout_t[other_at, :])
         act, slope = gelu_parts(pre)
         act = act.astype(bf16)
         gp = (ga * slope).astype(bf16)
-        po_send[index, 0] = mm(act, wout_v[:, other_at]).astype(bf16)
-        po_send[index, 1] = mm(gp, win_v[other_at, :], NT).astype(bf16)
-        give = remote(po_send.at[index], po_recv.at[index], 13 + index, 13 + index, others[0])
-        give.start()
-        acc[index, 0] = mm(act, wout_v[:, mine_at])
-        acc[index, 1] = mm(gp, win_v[mine_at, :], NT)
-        return give
-
-    to_core.wait_recv()
-    give0 = expert(d_own, d_core, 0)
-    to_chip.wait_recv()
-    forward = remote(d_chip, d_diag, 12, 12, others[0])
-    forward.start()
-    forward.wait_recv()
-    give1 = expert(d_chip, d_diag, 1)
-    give1.wait_recv()
-    xs_send[...] = (acc[1] + po_recv[1].astype(f32)).astype(bf16)
-    cross = remote(xs_send, xs_recv, 15, 15, others[1])
-    cross.start()
-    give0.wait_recv()
-    total = acc[0] + po_recv[0].astype(f32)
-    cross.wait_recv()
-    total = (total + xs_recv[...].astype(f32)).astype(bf16)
-    send_b[...] = jnp.stack([total[0], total[1]], axis=1)
-
-    own_b = spread(send_b, rows_b, 1)
+        shape = (2, size, half)
+        po_send[c, 0] = mm(act, wout_v[:, other_at]).astype(bf16).reshape(shape)
+        po_send[c, 1] = mm(gp, win_t[:, other_at]).astype(bf16).reshape(shape)
+        give[c].start()
+        acc[c, 0] = mm(act, wout_v[:, mine_at]).reshape(shape)
+        acc[c, 1] = mm(gp, win_t[:, mine_at]).reshape(shape)
+
+    def reduce(c):
+        give[c].wait_recv()
+        xs_send[c] = (acc[c, :, 1] + po_recv[c, :, 1].astype(f32)).astype(bf16)
+        cross[c].start()
+
+    def finish(c):
+        total = acc[c, :, 0] + po_recv[c, :, 0].astype(f32)
+        cross[c].wait_recv()
+        total = (total + xs_recv[c].astype(f32)).astype(bf16)
+        send_b[piece(c)] = jnp.stack([total[0], total[1]], axis=1)
+        if c == 0:
+            own_b.start()
+        back_chunk(c)
+
+    out_chunk(0)
+    for slot in range(chunks + 3):
+        if slot + 1 < chunks:
+            out_chunk(slot + 1)
+        for lag, stage in ((0, arrive), (1, share), (2, reduce), (3, finish), (1, expert)):
+            if 0 <= slot - lag < chunks:
+                stage(slot - lag)
+
     own_b.wait()
     wait_all(rows_b, n - 1, wsem.at[3])
 
@@ -229,8 +270,8 @@
     ef[k] = mm(gl, tok2, TN)
     ef[1 - k] = mm(gl, tok_o[...].reshape(4 * tk, half), TN)
     hn = n // 2
-    mine = pl.ds(pl.multiple_of(k * hn, hn), hn)
-    send_e[...] = jnp.stack([ef[0, mine, :].astype(bf16), ef[1, mine, :].astype(bf16)], axis=1)
+    part = pl.ds(pl.multiple_of(k * hn, hn), hn)
+    send_e[...] = jnp.stack([ef[0, part, :].astype(bf16), ef[1, part, :].astype(bf16)], axis=1)
     keeper = k == g // hn
     own_e = pltpu.make_async_copy(send_e.at[lax.rem(g, hn)], recv_e.at[g], lsem.at[8])
 
@@ -244,11 +285,11 @@
             device_id_type=MESH,
         ).start()
 
-    def piece(s, carry):
+    def step_e(s, carry):
         send_piece(s)
         return carry
 
-    lax.fori_loop(1, hn, piece, 0)
+    lax.fori_loop(1, hn, step_e, 0)
 
     @pl.when(keeper)
     def _():
@@ -303,9 +344,7 @@
     own_t.wait()
     for copy in gt_c:
         copy.wait_recv()
-    for copy in lg_c + tok_c + go_c + gt_c + [
-        tok_x, to_chip, to_core, give0, give1, forward, cross, gl_x
-    ]:
+    for copy in lg_c + tok_c + go_c + gt_c + to_chip + to_core + give + cross + [tok_x, gl_x]:
         copy.wait_send()
     wait_all(send_f, n - 1, wsem.at[0])
     wait_all(send_b, n - 1, wsem.at[2])
@@ -315,6 +354,8 @@
     images, tk, width = tokens.shape
     ff = w_in.shape[2]
     half = width // 2
+    chunks = 4
+    size = n // chunks
     hbm = pl.BlockSpec(memory_space=pltpu.HBM)
     vm = pltpu.VMEM
     scratch = [
@@ -323,16 +364,18 @@
         vm((4, tk, half), bf16), vm((4, tk, half), bf16), vm((4, tk, half), bf16),
         vm((4 * tk, n), f32), vm((4 * tk, n), f32),
         vm((n, 2, half), bf16), vm((n, 2, half), bf16),
-        vm((2, n, half), bf16), vm((2, n, half), bf16), vm((2, n, half), bf16),
-        vm((2, n, half), bf16),
-        vm((2, 2, n, half), bf16), vm((2, 2, n, half), bf16), vm((2, 2, n, half), f32),
-        vm((2, n, half), bf16), vm((2, n, half), bf16),
+        vm((chunks, 2, 2, size, half), bf16), vm((chunks, 2, 2, size, half), bf16),
+        vm((ff, width), bf16), vm((width, ff), bf16),
+        vm((chunks, 2, 2, size, half), bf16), vm((chunks, 2, 2, size, half), bf16),
+        vm((chunks, 2, 2, size, half), f32),
+        vm((chunks, 2, size, half), bf16), vm((chunks, 2, size, half), bf16),
         vm((n, 2, half), bf16), vm((n, 2, half), bf16),
         vm((4 * tk, n), f32), vm((4 * tk, n), f32), vm((4, tk, half), bf16),
         vm((2, n, half), f32), vm((n // 2, 2, half), bf16), vm((n, 2, half), bf16),
         vm((2, 2, half), f32),
-        pltpu.SemaphoreType.DMA((10,)), pltpu.SemaphoreType.DMA((25,)),
-        pltpu.SemaphoreType.DMA((25,)), pltpu.SemaphoreType.DMA((6,)),
+        pltpu.SemaphoreType.DMA((10,)), pltpu.SemaphoreType.DMA((70,)),
+        pltpu.SemaphoreType.DMA((70,)), pltpu.SemaphoreType.DMA((6,)),
+        pltpu.SemaphoreType.DMA((chunks,)),
         pltpu.SemaphoreType.REGULAR((2,)),
     ]
     stride = 37 if n == 128 else 1

time: 93.6 us -> 88.6 us (0.947)
  Pallas kernels: 89.8 us -> 84.8 us
    pallas_call x1, Pallas kernels: 89.8 us -> 84.8 us  [shards(): pl.pallas_call(functools.partial(kernel, n, nz, stride), out_shape=(jax.S...]
where the time goes in v3:
time: 88.6 us; the launch traced here: 88.4 us
  Pallas kernels  84.8 us (96%)
  local copies, waits for them, and re-layouts  2.96 us (3%)
    pallas_call x1, Pallas kernels, shards(): pl.pallas_call(functools.partial(kernel, n, nz, stride), out_shape=(jax.S...  84.8 us
    unnamed x2, local copies, waits for them, and re-layouts  2.96 us

profile of v3, /device:TPU:1, one launch (start us, length us, event | category | flops | bytes accessed | tf_op | source)
XLA Modules:
  0.0 88.4 jit_solution(17471866349457216056)
XLA Ops:
  0.6 84.8 %shard_map.68 = (bf16[2,64,1280]{2,1,0:T(8,128)(2,1)}, f32[1,320]{1,0:T(1,128)}) custom-call(bf16[2,64,1280]{2,1,0:T(8,128)(2,1)} %tok_hbm.1, bf16[128,1280]{1,0:T(8,128)(2,1)} %emb_hbm.1, bf16[1,1280,640]{2,1,0:T(8,128)(2,1)} %win_hbm.1, bf16[1,640,1280]{2,1,0:T(8,128)(2,1)} %wout_hbm.1, bf16[2,64,1280]{2,1,0:T(8,128)(2,1)} %go_hbm.1), custom_call_target="tpu_custom_call" | custom-call | flops 2000000000 | bytes 6000000 | tf_op jit(solution)/shard_map/pallas_call | solution.py:383
  85.5 1.7 %copy.9 = bf16[2,64,1280]{2,1,0:T(8,128)(2,1)} copy(bf16[2,64,1280]{2,1,0:T(8,128)(2,1)} %get-tuple-element.4) | data formatting | bytes 655360
  87.2 1.2 %copy.10 = f32[1,320]{1,0:T(1,128)} copy(f32[1,320]{1,0:T(1,128)} %get-tuple-element.5) | data formatting | bytes 2560

commit v4 on v3

--- a/solution.py
+++ b/solution.py
@@ -28,7 +28,7 @@
 
 def kernel(
     n, nz, stride, tok_hbm, emb_hbm, win_hbm, wout_hbm, go_hbm, gt_out, ge_out,
-    tok_v, emb_v, win_v, wout_v, lg_own, lg, tok_d, go_d, tok_o,
+    emb_v, win_v, wout_v, lg_own, lg, tok_d, go_d, tok_o,
     disp_v, comb_v, send_f, rows_f, mine, other, win_t, wout_t,
     po_send, po_recv, acc, xs_send, xs_recv, send_b, rows_b,
     gl_send, gl_recv, gt_send, ef, send_e, recv_e, fin, lsem, ssem, rsem, wsem, fsem, here,
@@ -59,15 +59,15 @@
         return t, 2 * (j + odd - 2 * j * odd) + k
 
     loads = [
-        pltpu.make_async_copy(tok_hbm, tok_v, lsem.at[0]),
+        None,
         pltpu.make_async_copy(emb_hbm, emb_v, lsem.at[1]),
         pltpu.make_async_copy(win_hbm.at[0], win_v, lsem.at[2]),
         pltpu.make_async_copy(wout_hbm.at[0], wout_v, lsem.at[3]),
         pltpu.make_async_copy(tok_hbm.at[j, :, cols(k)], tok_d.at[h], lsem.at[4]),
         pltpu.make_async_copy(go_hbm.at[j, :, cols(k)], go_d.at[h], lsem.at[5]),
     ]
-    for load in loads:
-        load.start()
+    for i in (4, 1, 5, 2, 3):
+        loads[i].start()
 
     zy = n // 2
     ny = zy // nz
@@ -86,25 +86,9 @@
     for peer in direct:
         tell(barrier, peer)
 
-    loads[0].wait()
-    loads[1].wait()
-    for image in range(2):
-        lg_own[image] = mm(tok_v[image], emb_v[...], NT)
-    lg[h] = lg_own[j]
-    loads[2].wait()
-    win_t[...] = win_v[...].T
-    loads[3].wait()
-    wout_t[...] = wout_v[...].T
     pl.semaphore_wait(barrier, len(direct))
-    for peer in along_z:
-        tell(here.at[0], peer)
-
-    tok_c, lg_c, go_c = [], [], []
-    for i in (1, 2, 0):
-        where = others[i]
-        copy = remote(lg_own.at[where[0]], lg.at[h], i, i, where)
-        copy.start()
-        lg_c.append(copy)
+
+    tok_c, go_c = [], []
     for i in (1, 2, 0):
         where = others[i]
         copy = remote(tok_hbm.at[where[0], :, cols(where[1])], tok_d.at[h], 3 + i, 3 + i, where)
@@ -115,10 +99,26 @@
         copy = remote(go_hbm.at[where[0], :, cols(where[1])], go_d.at[h], 6 + i, 6 + i, where)
         copy.start()
         go_c.append(copy)
-
-    for copy in lg_c:
+    for peer in along_z:
+        tell(here.at[0], peer)
+    pl.semaphore_wait(here.at[0], nz - 1)
+    tell(here.at[1], along_x)
+    loads[1].wait()
+    loads[2].wait()
+    win_t[...] = win_v[...].T
+    loads[3].wait()
+    wout_t[...] = wout_v[...].T
+
+    for copy in tok_c:
         copy.wait_recv()
-    logits = lg[...].reshape(4 * tk, n)
+    loads[4].wait()
+    lg_own[...] = mm(tok_d[...].reshape(4 * tk, half), emb_v[:, cols(k)], NT)
+    lg_x = remote(lg_own, lg, 0, 0, others[0])
+    lg_x.start()
+    tok_x = remote(tok_d, tok_o, 9, 9, others[0])
+    tok_x.start()
+    lg_x.wait_recv()
+    logits = lg_own[...] + lg[...]
     col = jnp.exp(logits - jnp.max(logits, axis=0, keepdims=True))
     disp = col / jnp.sum(col, axis=0, keepdims=True)
     row = jnp.exp(logits - jnp.max(logits, axis=1, keepdims=True))
@@ -126,21 +126,12 @@
     disp_v[...] = disp
     comb_v[...] = comb
 
-    for copy in tok_c:
-        copy.wait_recv()
-    loads[4].wait()
-    tok_x = remote(tok_d, tok_o, 9, 9, others[0])
-    tok_x.start()
     slot_rows = mm(disp.astype(bf16), tok_d[...].reshape(4 * tk, half), TN).astype(bf16)
     for copy in go_c:
         copy.wait_recv()
     loads[5].wait()
     grad_rows = mm(comb.astype(bf16), go_d[...].reshape(4 * tk, half), TN).astype(bf16)
     send_f[...] = jnp.stack([slot_rows, grad_rows], axis=1)
-
-    if nz > 1:
-        pl.semaphore_wait(here.at[0], nz - 1)
-    tell(here.at[1], along_x)
     pl.semaphore_wait(here.at[1], 1)
 
     def wait_all(ref, count, sem):
@@ -238,13 +229,13 @@
             own_b.start()
         back_chunk(c)
 
-    out_chunk(0)
-    for slot in range(chunks + 3):
-        if slot + 1 < chunks:
-            out_chunk(slot + 1)
-        for lag, stage in ((0, arrive), (1, share), (2, reduce), (3, finish), (1, expert)):
-            if 0 <= slot - lag < chunks:
-                stage(slot - lag)
+    for c in range(chunks):
+        out_chunk(c)
+    order = [(arrive, 0), (arrive, 1), (arrive, 2), (arrive, 3), (share, 0), (share, 1), (expert, 0), (share, 2),
+             (expert, 1), (reduce, 0), (share, 3), (expert, 2), (reduce, 1), (expert, 3), (finish, 0), (reduce, 2),
+             (finish, 1), (reduce, 3), (finish, 2), (finish, 3)]
+    for stage, c in order:
+        stage(c)
 
     own_b.wait()
     wait_all(rows_b, n - 1, wsem.at[3])
@@ -344,7 +335,7 @@
     own_t.wait()
     for copy in gt_c:
         copy.wait_recv()
-    for copy in lg_c + tok_c + go_c + gt_c + to_chip + to_core + give + cross + [tok_x, gl_x]:
+    for copy in tok_c + go_c + gt_c + to_chip + to_core + give + cross + [lg_x, tok_x, gl_x]:
         copy.wait_send()
     wait_all(send_f, n - 1, wsem.at[0])
     wait_all(send_b, n - 1, wsem.at[2])
@@ -359,8 +350,8 @@
     hbm = pl.BlockSpec(memory_space=pltpu.HBM)
     vm = pltpu.VMEM
     scratch = [
-        vm((images, tk, width), bf16), vm((n, width), bf16), vm((width, ff), bf16),
-        vm((ff, width), bf16), vm((images, tk, n), f32), vm((4, tk, n), f32),
+        vm((n, width), bf16), vm((width, ff), bf16),
+        vm((ff, width), bf16), vm((4 * tk, n), f32), vm((4 * tk, n), f32),
         vm((4, tk, half), bf16), vm((4, tk, half), bf16), vm((4, tk, half), bf16),
         vm((4 * tk, n), f32), vm((4 * tk, n), f32),
         vm((n, 2, half), bf16), vm((n, 2, half), bf16),
@@ -380,14 +371,16 @@
     ]
     stride = 37 if n == 128 else 1
     nz = 8 if n == 128 else 2
+    results = (
+        jax.ShapeDtypeStruct(tokens.shape, bf16),
+        jax.ShapeDtypeStruct((1, width // 4), f32),
+    )
+    whole = pl.BlockSpec(memory_space=pltpu.VMEM)
     return pl.pallas_call(
         functools.partial(kernel, n, nz, stride),
-        out_shape=(
-            jax.ShapeDtypeStruct(tokens.shape, bf16),
-            jax.ShapeDtypeStruct((1, width // 4), f32),
-        ),
+        out_shape=results,
         in_specs=[hbm] * 5,
-        out_specs=(hbm, pl.BlockSpec(memory_space=pltpu.VMEM)),
+        out_specs=(hbm, whole),
         scratch_shapes=scratch,
         compiler_params=pltpu.CompilerParams(
             collective_id=0, has_side_effects=True, vmem_limit_bytes=60 * 2**20
@@ -396,8 +389,6 @@
             flops=2 * 10**9, bytes_accessed=6 * 10**6, transcendentals=10**6
         ),
     )(tokens, slot_embed, w_in, w_out, grad_out)
-
-
 def solution(mesh):
     return jax.shard_map(
         functools.partial(shards, mesh.shape["expert"]),

time: 88.6 us -> 79.5 us (0.90)
  Pallas kernels: 84.8 us -> 75.5 us
    pallas_call x1, Pallas kernels: 84.8 us -> 75.5 us  [shards(): pl.pallas_call(functools.partial(kernel, n, nz, stride), out_shape=result...]
where the time goes in v4:
time: 79.5 us; the launch traced here: 79.1 us
  Pallas kernels  75.5 us (95%)
  local copies, waits for them, and re-layouts  2.96 us (4%)
    pallas_call x1, Pallas kernels, shards(): pl.pallas_call(functools.partial(kernel, n, nz, stride), out_shape=result...  75.5 us
    unnamed x2, local copies, waits for them, and re-layouts  2.96 us

profile of v4, /device:TPU:1, one launch (start us, length us, event | category | flops | bytes accessed | tf_op | source)
XLA Modules:
  0.0 79.1 jit_solution(15064970722863086835)
XLA Ops:
  0.6 75.5 %shard_map.68 = (bf16[2,64,1280]{2,1,0:T(8,128)(2,1)}, f32[1,320]{1,0:T(1,128)}) custom-call(bf16[2,64,1280]{2,1,0:T(8,128)(2,1)} %tok_hbm.1, bf16[128,1280]{1,0:T(8,128)(2,1)} %emb_hbm.1, bf16[1,1280,640]{2,1,0:T(8,128)(2,1)} %win_hbm.1, bf16[1,640,1280]{2,1,0:T(8,128)(2,1)} %wout_hbm.1, bf16[2,64,1280]{2,1,0:T(8,128)(2,1)} %go_hbm.1), custom_call_target="tpu_custom_call" | custom-call | flops 2000000000 | bytes 6000000 | tf_op jit(solution)/shard_map/pallas_call | solution.py:379
  76.1 1.7 %copy.9 = bf16[2,64,1280]{2,1,0:T(8,128)(2,1)} copy(bf16[2,64,1280]{2,1,0:T(8,128)(2,1)} %get-tuple-element.4) | data formatting | bytes 655360
  77.8 1.2 %copy.10 = f32[1,320]{1,0:T(1,128)} copy(f32[1,320]{1,0:T(1,128)} %get-tuple-element.5) | data formatting | bytes 2560

commit v5 on v4

--- a/solution.py
+++ b/solution.py
@@ -133,6 +133,7 @@
     grad_rows = mm(comb.astype(bf16), go_d[...].reshape(4 * tk, half), TN).astype(bf16)
     send_f[...] = jnp.stack([slot_rows, grad_rows], axis=1)
     pl.semaphore_wait(here.at[1], 1)
+    tell(here.at[2], device(others[0]))
 
     def wait_all(ref, count, sem):
         part = ref.at[pl.ds(0, count)]
@@ -170,20 +171,19 @@
             ).start()
             return carry
 
-        lax.fori_loop(max(chunk * size, 1), (chunk + 1) * size, step, 0)
-
-    to_chip = [
-        remote(mine.at[c, :, 0], mine.at[c, :, 1], 30 + c, 30 + c, others[1]) for c in range(chunks)
-    ]
-    to_core = [
-        remote(mine.at[c], other.at[c], 40 + c, 40 + c, others[0]) for c in range(chunks)
-    ]
-    give = [
-        remote(po_send.at[c], po_recv.at[c], 50 + c, 50 + c, others[0]) for c in range(chunks)
-    ]
-    cross = [
-        remote(xs_send.at[c], xs_recv.at[c], 60 + c, 60 + c, others[1]) for c in range(chunks)
-    ]
+        lax.fori_loop(jnp.maximum(chunk * size, 1), (chunk + 1) * size, step, 0)
+
+    def to_chip(c):
+        return remote(mine.at[c, :, 0], mine.at[c, :, 1], 30 + c, 30 + c, others[1])
+
+    def to_core(c):
+        return remote(mine.at[c], other.at[c], 40 + c, 40 + c, others[0])
+
+    def give(c):
+        return remote(po_send.at[c], po_recv.at[c], 50 + c, 50 + c, others[0])
+
+    def cross(c):
+        return remote(xs_send.at[c], xs_recv.at[c], 60 + c, 60 + c, others[1])
 
     def arrive(c):
         if c == 0:
@@ -191,14 +191,14 @@
         wait_all(rows_f, size - (c == 0), fsem.at[c])
         mine[c, 0, 0] = rows_f[piece(c), 0, :]
         mine[c, 1, 0] = rows_f[piece(c), 1, :]
-        to_chip[c].start()
+        to_chip(c).start()
 
     def share(c):
-        to_chip[c].wait_recv()
-        to_core[c].start()
+        to_chip(c).wait_recv()
+        to_core(c).start()
 
     def expert(c):
-        to_core[c].wait_recv()
+        to_core(c).wait_recv()
         mine0 = mine[c, 0].reshape(2 * size, half)
         mine1 = mine[c, 1].reshape(2 * size, half)
         other0 = other[c, 0].reshape(2 * size, half)
@@ -211,32 +211,37 @@
         shape = (2, size, half)
         po_send[c, 0] = mm(act, wout_v[:, other_at]).astype(bf16).reshape(shape)
         po_send[c, 1] = mm(gp, win_t[:, other_at]).astype(bf16).reshape(shape)
-        give[c].start()
+        give(c).start()
         acc[c, 0] = mm(act, wout_v[:, mine_at]).reshape(shape)
         acc[c, 1] = mm(gp, win_t[:, mine_at]).reshape(shape)
 
     def reduce(c):
-        give[c].wait_recv()
+        give(c).wait_recv()
         xs_send[c] = (acc[c, :, 1] + po_recv[c, :, 1].astype(f32)).astype(bf16)
-        cross[c].start()
+        cross(c).start()
 
     def finish(c):
         total = acc[c, :, 0] + po_recv[c, :, 0].astype(f32)
-        cross[c].wait_recv()
+        cross(c).wait_recv()
         total = (total + xs_recv[c].astype(f32)).astype(bf16)
         send_b[piece(c)] = jnp.stack([total[0], total[1]], axis=1)
-        if c == 0:
-            own_b.start()
         back_chunk(c)
 
     for c in range(chunks):
         out_chunk(c)
-    order = [(arrive, 0), (arrive, 1), (arrive, 2), (arrive, 3), (share, 0), (share, 1), (expert, 0), (share, 2),
-             (expert, 1), (reduce, 0), (share, 3), (expert, 2), (reduce, 1), (expert, 3), (finish, 0), (reduce, 2),
-             (finish, 1), (reduce, 3), (finish, 2), (finish, 3)]
-    for stage, c in order:
-        stage(c)
-
+    for c in range(chunks):
+        arrive(c)
+
+    def slot(i, carry):
+        for stage, lag in ((share, 0), (expert, 1), (finish, 4), (reduce, 2)):
+            @pl.when(jnp.logical_and(i >= lag, i < chunks + lag))
+            def _(stage=stage, lag=lag):
+                stage(i - lag)
+
+        return carry
+
+    lax.fori_loop(0, chunks + 4, slot, 0)
+    own_b.start()
     own_b.wait()
     wait_all(rows_b, n - 1, wsem.at[3])
 
@@ -264,15 +269,16 @@
     part = pl.ds(pl.multiple_of(k * hn, hn), hn)
     send_e[...] = jnp.stack([ef[0, part, :].astype(bf16), ef[1, part, :].astype(bf16)], axis=1)
     keeper = k == g // hn
-    own_e = pltpu.make_async_copy(send_e.at[lax.rem(g, hn)], recv_e.at[g], lsem.at[8])
+    own_e = pltpu.make_async_copy(send_e.at[lax.rem(g, hn)], recv_e.at[lax.rem(g, hn)], lsem.at[8])
+    pl.semaphore_wait(here.at[2], 1)
 
     def send_piece(s):
         e = lax.rem(g + lax.rem(s * stride, hn), hn)
         t = k * hn + e
         odd = lax.rem(s, 2)
         pltpu.make_async_remote_copy(
-            src_ref=send_e.at[e], dst_ref=recv_e.at[g], send_sem=wsem.at[4],
-            recv_sem=wsem.at[5], device_id=(t, 2 * (j + odd - 2 * j * odd) + k),
+            src_ref=send_e.at[e], dst_ref=recv_e.at[lax.rem(g, hn)], send_sem=wsem.at[4],
+            recv_sem=wsem.at[5], device_id=(t, 2 * (j + odd - 2 * j * odd) + g // hn),
             device_id_type=MESH,
         ).start()
 
@@ -303,31 +309,28 @@
         copy.start()
         gt_c.append(copy)
 
-    fin_c = [remote(fin.at[j], fin.at[j], 20 + i, 23 + j, others[i]) for i in range(3)]
-
     @pl.when(keeper)
     def _():
         own_e.wait()
-        wait_all(recv_e, n - 1, wsem.at[5])
-        rows = recv_e[...].reshape(2 * n, half)
-        shape = (8, 2 * n)
-        pick = lax.rem(lax.broadcasted_iota(jnp.int32, shape, 1), 2)
-        pick = (pick == lax.broadcasted_iota(jnp.int32, shape, 0)).astype(bf16)
-        fin[j] = mm(pick, rows)[0:2, :]
-        for copy in fin_c:
-            copy.start()
-        for copy in fin_c:
-            copy.wait_send()
+        wait_all(recv_e, hn - 1, wsem.at[5])
         wait_all(send_e, hn - 1, wsem.at[4])
-        pltpu.make_async_copy(fin.at[1 - j], fin.at[1 - j], rsem.at[24 - j]).wait()
 
     @pl.when(jnp.logical_not(keeper))
     def _():
+        wait_all(recv_e, hn, wsem.at[5])
         wait_all(send_e, hn, wsem.at[4])
-        for chip in range(2):
-            pltpu.make_async_copy(fin.at[chip], fin.at[chip], rsem.at[23 + chip]).wait()
-
-    both = fin[0] + fin[1]
+
+    rows = recv_e[...].reshape(2 * hn, half)
+    shape = (8, 2 * hn)
+    pick = lax.rem(lax.broadcasted_iota(jnp.int32, shape, 1), 2)
+    pick = (pick == lax.broadcasted_iota(jnp.int32, shape, 0)).astype(bf16)
+    fin[h] = mm(pick, rows)[0:2, :]
+    fin_c = [remote(fin.at[h], fin.at[h], 20 + i, 23 + i, others[i]) for i in range(3)]
+    for copy in fin_c:
+        copy.start()
+    for copy in fin_c:
+        copy.wait()
+    both = (fin[0] + fin[1]) + (fin[2] + fin[3])
     row = jnp.where(j == 0, both[0:1, :], both[1:2, :])
     quarter = half // 2
     ge_out[...] = jnp.where(k == 0, row[:, :quarter], row[:, quarter:])
@@ -335,8 +338,11 @@
     own_t.wait()
     for copy in gt_c:
         copy.wait_recv()
-    for copy in tok_c + go_c + gt_c + to_chip + to_core + give + cross + [lg_x, tok_x, gl_x]:
+    for copy in tok_c + go_c + gt_c + [lg_x, tok_x, gl_x]:
         copy.wait_send()
+    for c in range(chunks):
+        for copy in (to_chip(c), to_core(c), give(c), cross(c)):
+            copy.wait_send()
     wait_all(send_f, n - 1, wsem.at[0])
     wait_all(send_b, n - 1, wsem.at[2])
 
@@ -362,12 +368,12 @@
         vm((chunks, 2, size, half), bf16), vm((chunks, 2, size, half), bf16),
         vm((n, 2, half), bf16), vm((n, 2, half), bf16),
         vm((4 * tk, n), f32), vm((4 * tk, n), f32), vm((4, tk, half), bf16),
-        vm((2, n, half), f32), vm((n // 2, 2, half), bf16), vm((n, 2, half), bf16),
-        vm((2, 2, half), f32),
+        vm((2, n, half), f32), vm((n // 2, 2, half), bf16), vm((n // 2, 2, half), bf16),
+        vm((4, 2, half), f32),
         pltpu.SemaphoreType.DMA((10,)), pltpu.SemaphoreType.DMA((70,)),
         pltpu.SemaphoreType.DMA((70,)), pltpu.SemaphoreType.DMA((6,)),
         pltpu.SemaphoreType.DMA((chunks,)),
-        pltpu.SemaphoreType.REGULAR((2,)),
+        pltpu.SemaphoreType.REGULAR((3,)),
     ]
     stride = 37 if n == 128 else 1
     nz = 8 if n == 128 else 2
@@ -383,7 +389,7 @@
         out_specs=(hbm, whole),
         scratch_shapes=scratch,
         compiler_params=pltpu.CompilerParams(
-            collective_id=0, has_side_effects=True, vmem_limit_bytes=60 * 2**20
+            collective_id=0, has_side_effects=True, vmem_limit_bytes=107 * 2**19
         ),
         cost_estimate=pl.CostEstimate(
             flops=2 * 10**9, bytes_accessed=6 * 10**6, transcendentals=10**6

time: 79.5 us -> 76.1 us (0.957)
  local copies, waits for them, and re-layouts: 2.96 us -> 1.29 us
  Pallas kernels: 75.5 us -> 74.1 us
    unnamed x2, local copies, waits for them, and re-layouts: 2.96 us -> 1.29 us
    pallas_call x1, Pallas kernels: 75.5 us -> 74.1 us  [shards(): pl.pallas_call(functools.partial(kernel, n, nz, stride), out_shape=result...]
where the time goes in v5:
time: 76.1 us; the launch traced here: 76 us
  Pallas kernels  74.1 us (97%)
  local copies, waits for them, and re-layouts  1.29 us (2%)
    pallas_call x1, Pallas kernels, shards(): pl.pallas_call(functools.partial(kernel, n, nz, stride), out_shape=result...  74.1 us

profile of v5, /device:TPU:1, one launch (start us, length us, event | category | flops | bytes accessed | tf_op | source)
XLA Modules:
  0.0 76.0 jit_solution(14457067555141012283)
XLA Ops:
  0.6 74.1 %shard_map.68 = (bf16[2,64,1280]{2,1,0:T(8,128)(2,1)S(1)}, f32[1,320]{1,0:T(1,128)S(1)}) custom-call(bf16[2,64,1280]{2,1,0:T(8,128)(2,1)} %tok_hbm.1, bf16[128,1280]{1,0:T(8,128)(2,1)} %emb_hbm.1, bf16[1,1280,640]{2,1,0:T(8,128)(2,1)} %win_hbm.1, bf16[1,640,1280]{2,1,0:T(8,128)(2,1)} %wout_hbm.1, bf16[2,64,1280]{2,1,0:T(8,128)(2,1)} %go_hbm.1), custom_call_target="tpu_custom_call" | custom-call | flops 2000000000 | bytes 6000000 | tf_op jit(solution)/shard_map/pallas_call | solution.py:385
  74.7 0.7 copy.9
  75.5 0.6 copy.10
